TPU v7x, 128 devices: a whole 4x4x4 slice. The times are simulated.
128 devices in a mesh: ctx: 16 (over y_lo, z, core), head: 8 (over x, y_hi).
Axes of the slice: x: 4, y: 4 (y_hi: 2, y_lo: 2; y = y_hi * 2 + y_lo), z: 4, core: 2. Of those that a mesh axis runs over, the one named last changes fastest.
Arguments:
- queries: bfloat16 [2048, 36864], P('ctx', 'head'), may hold values from -296 to 296
- latent_keys: bfloat16 [2048, 576], P('ctx'), may hold values from -9 to 9
- block_order: int32 [16], replicated, may hold values from 0 to 15, each once
- out_grad: bfloat16 [2048, 32768], P('ctx', 'head'), may hold values from -6 to 6
Outputs:
- attended: bfloat16 [2048, 32768], P('ctx', 'head')
- query_grad: bfloat16 [2048, 36864], P('ctx', 'head')
- latent_grad: bfloat16 [2048, 576], P('ctx')
Inputs may be any that keep to these rules, and one draw needn't show every extreme that they name: `block_order`: a permutation: each block index once.
All inputs are finite; a program needn't handle non-finite values.
Results may differ from a plain program's by a relative error of at most 0.034.
Values may be sent and summed in bfloat16 or wider, within the bound.
A program may use at most 64 MiB of HBM per device.

v0:
```python
import jax
import jax.numpy as jnp
from jax import lax
from jax.sharding import PartitionSpec as P

LATENT = 512
ROPE = 64
score_scale = 192.0 ** (-0.5)
masked_value = -1e30


def row_positions(block_order, first_row, count, shard_rows):
    rows = first_row + jnp.arange(count, dtype=jnp.int32)
    owner = rows // shard_rows
    blocks = block_order.shape[0]
    onehot = (owner[:, None] == jnp.arange(blocks, dtype=jnp.int32)[None, :]).astype(jnp.int32)
    base = jnp.sum(onehot * block_order[None, :], axis=1)
    return base * shard_rows + rows % shard_rows


def local(queries, latent_keys, block_order, out_grad):
    kdim = LATENT + ROPE
    shard_rows = latent_keys.shape[0]
    head_count = queries.shape[1] // kdim
    query_three = queries.reshape(shard_rows, head_count, kdim)
    grad_three = out_grad.reshape(shard_rows, head_count, LATENT)
    own_index = lax.axis_index("ctx")
    query_pos = row_positions(block_order, own_index * shard_rows, shard_rows, shard_rows)

    def piece_scores(piece, start):
        score = (
            jnp.einsum("thd,pd->htp", query_three, piece, preferred_element_type=jnp.float32)
            * score_scale
        )
        key_pos = row_positions(block_order, start, piece.shape[0], shard_rows)
        visible = key_pos[None, :] <= query_pos[:, None]
        return (jnp.where(visible[None], score, masked_value), visible)

    running_max = jnp.full((head_count, shard_rows), masked_value, jnp.float32)
    score, visible = piece_scores(
        lax.all_gather(latent_keys, "ctx", axis=0, tiled=True), jnp.int32(0)
    )
    new_max = jnp.maximum(running_max, jnp.max(score, axis=2))
    weights = jnp.where(visible[None], jnp.exp(score - new_max[:, :, None]), 0.0)
    new_sum = jnp.sum(weights, axis=2)
    lse = new_max + jnp.log(new_sum)
    piece = lax.all_gather(latent_keys, "ctx", axis=0, tiled=True)
    score, visible = piece_scores(piece, jnp.int32(0))
    prob_b = jnp.where(visible[None], jnp.exp(score - lse[:, :, None]), 0.0).astype(jnp.bfloat16)
    accum = jnp.einsum("htp,pe->the", prob_b, piece[:, :LATENT], preferred_element_type=jnp.float32)
    attended = accum.astype(jnp.bfloat16)
    delta = jnp.sum(attended.astype(jnp.float32) * grad_three.astype(jnp.float32), axis=2).T
    piece = lax.all_gather(latent_keys, "ctx", axis=0, tiled=True)
    score, visible = piece_scores(piece, jnp.int32(0))
    prob = jnp.where(visible[None], jnp.exp(score - lse[:, :, None]), 0.0)
    prob_b = prob.astype(jnp.bfloat16)
    dprob = jnp.einsum(
        "the,pe->htp", grad_three, piece[:, :LATENT], preferred_element_type=jnp.float32
    )
    dscore = (prob * (dprob - delta[:, :, None])).astype(jnp.bfloat16)
    query_accum = jnp.einsum("htp,pd->thd", dscore, piece, preferred_element_type=jnp.float32)
    key_part = score_scale * jnp.einsum(
        "htp,thd->pd", dscore, query_three, preferred_element_type=jnp.float32
    )
    value_part = jnp.einsum("htp,the->pe", prob_b, grad_three, preferred_element_type=jnp.float32)
    term = key_part + jnp.pad(value_part, ((0, 0), (0, ROPE)))
    key_accum = term
    query_accum, key_accum = (query_accum, key_accum)
    query_grad = (
        (score_scale * query_accum).astype(jnp.bfloat16).reshape(shard_rows, head_count * kdim)
    )
    partial_rows = lax.psum_scatter(key_accum, "ctx", scatter_dimension=0, tiled=True)
    latent_grad = lax.psum(partial_rows, "head").astype(jnp.bfloat16)
    return (attended.reshape(shard_rows, head_count * LATENT), query_grad, latent_grad)


def solution(mesh):
    placed = (P("ctx", "head"), P("ctx", None), P(), P("ctx", "head"))
    return jax.shard_map(
        local,
        mesh=mesh,
        in_specs=placed,
        out_specs=(P("ctx", "head"), P("ctx", "head"), P("ctx", None)),
        check_vma=False,
    )
```

profile of v0, /device:TPU:0, one launch (start us, length us, event | category | flops | bytes accessed | tf_op | source)
XLA Modules:
  0.0 196.5 jit_solution(11976603212448171671)
XLA Ops:
  7.2 0.0 all-gather.2.cloned.1.call-start
  7.2 0.7 all-gather.2.cloned.1.call-update
  7.9 0.0 reduce-scatter.2.cloned.1.call-start
  8.0 1.6 copy.34
  9.6 1.3 copy.37
  10.9 0.7 copy.30
  11.7 0.1 select_reduce_fusion.2
  11.8 0.1 select_reduce_fusion.1
  11.9 0.3 broadcast_compare_fusion
  12.2 38.2 %all-gather.2.cloned.1.call-done = bf16[2048,576]{0,1:T(8,128)(2,1)} async-done(((bf16[128,576]{0,1:T(8,128)(2,1)}), bf16[2048,576]{0,1:T(8,128)(2,1)}) %all-gather.2.cloned.1.call-update) | async-done | bytes 2359312 | tf_op jit(solution)/shard_map/all_gather | solution.py:47
  50.5 5.6 %fusion.3 = (f32[8,128]{1,0:T(8,128)S(1)}, f32[2048,128,8]{1,0,2:T(8,128)S(1)}) fusion(pred[128,2048]{0,1:T(8,128)(4,1)S(1)} %broadcast_compare_fusion, bf16[128,8,576]{0,2,1:T(8,128)(2,1)S(1)} %bitcast.65, bf16[2048,576]{0,1:T(8,128)(2,1)} %all-gather.2.cloned.1.call-done), kind=kOutput, calls=%fused_computation.7 | convolution fusion | flops 2422209536 | bytes 12193792 | tf_op jit(solution)/shard_map/thd,pd->htp/dot_general | solution.py:32
  56.1 2.0 %select_reduce_fusion = f32[8,128]{1,0:T(8,128)S(1)} fusion(f32[2048,128,8]{1,0,2:T(8,128)S(1)} %get-tuple-element.13, f32[8,128]{1,0:T(8,128)S(1)} %broadcast_maximum_fusion, pred[128,2048]{0,1:T(8,128)(4,1)S(1)} %broadcast_compare_fusion), kind=kLoop, calls=%fused_computation.5 | loop fusion | flops 10484736 | bytes 8658944 | tf_op jit(solution)/shard_map/reduce_sum | solution.py:45
  58.2 2.7 %convolution_bitcast_fusion = f32[2048,512]{0,1:T(8,128)S(1)} fusion(bf16[128,8,512]{0,2,1:T(8,128)(2,1)S(1)} %bitcast.62, f32[2048,128,8]{1,0,2:T(8,128)S(1)} %get-tuple-element.13, f32[8,128]{1,0:T(8,128)S(1)} %log_add_fusion, pred[128,2048]{0,1:T(8,128)(4,1)S(1)} %broadcast_compare_fusion), kind=kOutput, calls=%fused_computation.10 | convolution fusion | flops 2157969408 | bytes 13897728 | tf_op jit(solution)/shard_map/htp,the->pe/dot_general | solution.py:65
  60.9 3.7 %multiply_reduce_fusion = (f32[128,8]{0,1:T(8,128)S(1)}, bf16[128,8,512]{2,0,1:T(8,128)(2,1)}) fusion(bf16[128,8,512]{2,0,1:T(8,128)(2,1)S(1)} %copy-done.1, bf16[2048,576]{0,1:T(8,128)(2,1)S(1)} %copy-done.4, f32[2048,128,8]{1,0,2:T(8,128)S(1)} %get-tuple-element.13, f32[8,128]{1,0:T(8,128)S(1)} %log_add_fusion, ...), kind=kOutput, calls=%fused_computation.17 | convolution fusion | flops 2160589824 | bytes 12853248 | tf_op jit(solution)/shard_map/htp,pe->the/dot_general | solution.py:50
  64.6 4.5 %fusion.1 = bf16[8,128,2048]{1,2,0:T(8,128)(2,1)S(1)} fusion(f32[2048,128,8]{1,0,2:T(8,128)S(1)} %get-tuple-element.13, bf16[128,8,512]{0,2,1:T(8,128)(2,1)S(1)} %bitcast.63, f32[8,128]{1,0:T(8,128)S(1)} %bitcast.68, f32[8,128]{1,0:T(8,128)S(1)} %log_add_fusion, pred[128,2048]{0,1:T(8,128)(4,1)S(1)} %broadcast_compare_fusion, bf16[2048,576]{0,1:T(8,128)(2,1)S(1)} %copy-done.4), kind=kOutput, calls=%fused_computation.2 | convolution fusion | flops 2162163712 | bytes 15998976 | tf_op jit(solution)/shard_map/the,pe->htp/dot_general | solution.py:57
  69.0 2.0 %copy-done.5 = bf16[8,128,2048]{1,2,0:T(8,128)(2,1)} copy-done((bf16[8,128,2048]{1,2,0:T(8,128)(2,1)}, bf16[8,128,2048]{1,2,0:T(8,128)(2,1)S(1)}, u32[]{:S(2)}) %copy-start.5) | copy-done | bytes 4194328
  71.0 4.3 %fusion.4 = f32[2048,576]{0,1:T(8,128)} fusion(f32[2048,512]{0,1:T(8,128)S(1)} %convolution_bitcast_fusion, bf16[8,128,2048]{1,2,0:T(8,128)(2,1)S(1)} %fusion.1, bf16[128,8,576]{0,2,1:T(8,128)(2,1)S(1)} %bitcast.66), kind=kOutput, calls=%fused_computation.9 | convolution fusion | flops 2418278400 | bytes 14286848 | tf_op jit(solution)/shard_map/htp,thd->pd/dot_general | solution.py:62
  75.4 1.2 copy-done.2
  76.6 0.7 copy.33
  77.2 1.3 copy.41
  78.6 5.5 %multiply_convert_fusion = bf16[8,128,576]{1,2,0:T(8,128)(2,1)S(1)} fusion(bf16[8,128,2048]{1,2,0:T(8,128)(2,1)} %copy-done.5, bf16[2048,576]{0,1:T(8,128)(2,1)} %all-gather.2.cloned.1.call-done), kind=kOutput, calls=%fused_computation.15 | convolution fusion | flops 2417098752 | bytes 7733248 | tf_op jit(solution)/shard_map/htp,pd->thd/dot_general | solution.py:61
  84.1 1.4 copy.42
  85.5 58.2 %reduce-scatter.2.cloned.1.call-done = f32[128,576]{0,1:T(8,128)} async-done(((f32[2048,576]{0,1:T(8,128)}), f32[128,576]{0,1:T(8,128)}) %reduce-scatter.2.cloned.1.call-update) | async-done | bytes 294928 | tf_op jit(solution)/shard_map/reduce_scatter | solution.py:72
  143.7 45.9 %all-reduce.2 = bf16[128,576]{0,1:T(8,128)(2,1)} all-reduce(f32[128,576]{0,1:T(8,128)} %reduce-scatter.2.cloned.1.call-done), channel_id=1, replica_groups=mesh['ctx'=16,'head'=8] {'head'}, use_global_device_ids=true, to_apply=%region_6.7 | all-reduce | flops 73728 | bytes 442368 | tf_op jit(solution)/shard_map/psum | solution.py:73
  (17 shorter events, 0.1 us)
Async XLA Ops:
  7.2 3.7 %copy-start = (bf16[128,4608]{1,0:T(8,128)(2,1)S(1)}, bf16[128,4608]{1,0:T(8,128)(2,1)}, u32[]{:S(2)}) copy-start(bf16[128,4608]{1,0:T(8,128)(2,1)} %param.4) | copy-start | bytes 3538948
  7.2 4.5 %copy-start.3 = (s32[16]{0:T(128)S(1)}, s32[16]{0:T(128)}, u32[]{:S(2)}) copy-start(s32[16]{0:T(128)} %param.6) | copy-start | bytes 196
  7.2 43.3 %all-gather.2.cloned.1.call-start = ((), (), s32[]{:S(2)}) async-start(), calls=%async_computation.1 | async-start | bytes 2506752 | tf_op jit(solution)/shard_map/all_gather | solution.py:47
  7.9 135.8 %reduce-scatter.2.cloned.1.call-start = ((), (), s32[]{:S(2)}) async-start(), calls=%async_computation.2 | async-start | bytes 5013504 | tf_op jit(solution)/shard_map/reduce_scatter | solution.py:72
  58.1 2.7 %copy-start.1 = (bf16[128,8,512]{2,0,1:T(8,128)(2,1)S(1)}, bf16[128,8,512]{2,0,1:T(8,128)(2,1)}, u32[]{:S(2)}) copy-start(bf16[128,8,512]{2,0,1:T(8,128)(2,1)} %copy.37) | copy-start | bytes 3145732
  58.2 2.7 %copy-start.4 = (bf16[2048,576]{0,1:T(8,128)(2,1)S(1)}, bf16[2048,576]{0,1:T(8,128)(2,1)}, u32[]{:S(2)}) copy-start(bf16[2048,576]{0,1:T(8,128)(2,1)} %all-gather.2.cloned.1.call-done) | copy-start | bytes 7077892
  69.0 2.0 %copy-start.5 = (bf16[8,128,2048]{1,2,0:T(8,128)(2,1)}, bf16[8,128,2048]{1,2,0:T(8,128)(2,1)S(1)}, u32[]{:S(2)}) copy-start(bf16[8,128,2048]{1,2,0:T(8,128)(2,1)S(1)} %fusion.1) | copy-start | bytes 12582916
  75.4 1.2 copy-start.2
Sparse Core Ops, SparseCore 0:
  9.6 40.7 all-gather.1
  75.5 68.1 reduce-scatter.1
where the time goes:
time: 197 us; the launch traced here: 196 us
  waiting for transfers between devices  97.2 us (49%)
  blocking collectives  45.9 us (23%)
  matrix products  26.2 us (13%)
  between operations  14.2 us (7%)
  local copies, waits for them, and re-layouts  10.3 us (5%)
  other arithmetic  2.6 us (1%)
    reduce_scatter x1, waiting for transfers between devices, local(): lax.psum_scatter(key_accum, 'ctx', scatter_dimension=0, tiled=True)  58.2 us
    psum x1, blocking collectives, local(): latent_grad = lax.psum(partial_rows, 'head').astype(jnp.bfloat16)  45.9 us
    all_gather x1, waiting for transfers between devices, local(): piece = lax.all_gather(latent_keys, 'ctx', axis=0, tiled=True)  38.2 us
    unnamed x16, local copies, waits for them, and re-layouts  8.29 us
    dot_general x1, matrix products, piece_scores(): jnp.einsum('thd,pd->htp', query_three, piece, preferred_element_type=jnp....  5.59 us
    dot_general x1, matrix products, local(): jnp.einsum('htp,pd->thd', dscore, piece, preferred_element_type=jnp.float32)  5.5 us
    dot_general x1, matrix products, local(): jnp.einsum('the,pe->htp', grad_three, piece[:, :LATENT], preferred_elemen...  4.47 us
    dot_general x1, matrix products, local(): jnp.einsum('htp,thd->pd', dscore, query_three, preferred_element_type=jnp...  4.31 us
  transfers between devices with their start and end apart: 2, of which 2 were waited for; matrix products, arithmetic and copies ran while one was open for 7% of the time, Pallas kernels for 0%

commit v1 on v0

--- a/solution.py
+++ b/solution.py
@@ -44,7 +44,9 @@
     weights = jnp.where(visible[None], jnp.exp(score - new_max[:, :, None]), 0.0)
     new_sum = jnp.sum(weights, axis=2)
     lse = new_max + jnp.log(new_sum)
-    piece = lax.all_gather(latent_keys, "ctx", axis=0, tiled=True)
+    piece = jnp.concatenate(
+        lax.all_to_all(jnp.stack([latent_keys] * lax.axis_size("ctx")), "ctx", 0, 0), axis=0
+    )
     score, visible = piece_scores(piece, jnp.int32(0))
     prob_b = jnp.where(visible[None], jnp.exp(score - lse[:, :, None]), 0.0).astype(jnp.bfloat16)
     accum = jnp.einsum("htp,pe->the", prob_b, piece[:, :LATENT], preferred_element_type=jnp.float32)

time: 197 us -> 227 us (1.15)
  local copies, waits for them, and re-layouts: 10.3 us -> 25.5 us
  matrix products: 26.2 us -> 37.7 us
  starting transfers between devices: 0.08 us -> 6.59 us
  waiting for transfers between devices: 97.2 us -> 93.6 us
    all_gather x1, waiting for transfers between devices: 38.2 us -> 1.92 us  [local(): lax.all_gather(latent_keys, 'ctx', axis=0, tiled=True)]
    all_to_all x0 -> x1, waiting for transfers between devices: none -> 31.6 us  [local(): lax.all_to_all(jnp.stack([latent_keys] * lax.axis_size('ctx')), 'ctx', 0, 0)]
    reshape x0 -> x2, local copies, waits for them, and re-layouts: none -> 6.73 us  [local(): jnp.concatenate(lax.all_to_all(jnp.stack([latent_keys] * lax.axis_size('c...]
    all_to_all x0 -> x1, starting transfers between devices: none -> 6.51 us  [local(): lax.all_to_all(jnp.stack([latent_keys] * lax.axis_size('ctx')), 'ctx', 0, 0)]
    dot_general x1, matrix products: 3.67 us -> 9.94 us  [local(): jnp.einsum('htp,pe->the', prob_b, piece[:, :LATENT], preferred_element_ty...]
    all_to_all x0 -> x1, local copies, waits for them, and re-layouts: none -> 2.94 us  [local(): lax.all_to_all(jnp.stack([latent_keys] * lax.axis_size('ctx')), 'ctx', 0, 0)]
    another operation x0 -> x1, local copies, waits for them, and re-layouts: none -> 2.79 us  [local(): jnp.stack([latent_keys] * lax.axis_size('ctx'))]
    dot_general x1, matrix products: 4.47 us -> 7.25 us  [local(): jnp.einsum('the,pe->htp', grad_three, piece[:, :LATENT], preferred_elemen...]
  transfers between devices with their start and end apart: 2 -> 3, of which waited for: 2 -> 3; matrix products, arithmetic and copies ran while one was open for 7% -> 12% of each run, Pallas kernels for 0% -> 0%
where the time goes in v1:
time: 227 us
  waiting for transfers between devices  93.6 us (41%)
  blocking collectives  45.8 us (20%)
  matrix products  37.7 us (17%)
  local copies, waits for them, and re-layouts  25.5 us (11%)
  between operations  14.2 us (6%)
  starting transfers between devices  6.59 us (3%)
  other arithmetic  3.48 us (2%)
    reduce_scatter x1, waiting for transfers between devices, local(): lax.psum_scatter(key_accum, 'ctx', scatter_dimension=0, tiled=True)  59.4 us
    psum x1, blocking collectives, local(): latent_grad = lax.psum(partial_rows, 'head').astype(jnp.bfloat16)  45.8 us
    all_to_all x1, waiting for transfers between devices, local(): lax.all_to_all(jnp.stack([latent_keys] * lax.axis_size('ctx')), 'ctx', 0, 0)  31.6 us
    unnamed x20, local copies, waits for them, and re-layouts  11 us
    dot_general x1, matrix products, local(): jnp.einsum('htp,pe->the', prob_b, piece[:, :LATENT], preferred_element_ty...  9.94 us
    dot_general x1, matrix products, local(): jnp.einsum('the,pe->htp', grad_three, piece[:, :LATENT], preferred_elemen...  7.25 us
    reshape x2, local copies, waits for them, and re-layouts, local(): jnp.concatenate(lax.all_to_all(jnp.stack([latent_keys] * lax.axis_size('c...  6.73 us
    all_to_all x1, starting transfers between devices, local(): lax.all_to_all(jnp.stack([latent_keys] * lax.axis_size('ctx')), 'ctx', 0, 0)  6.51 us
  transfers between devices with their start and end apart: 3, of which 3 were waited for; matrix products, arithmetic and copies ran while one was open for 12% of the time, Pallas kernels for 0%

profile of v1, /device:TPU:0, one launch (start us, length us, event | category | flops | bytes accessed | tf_op | source)
XLA Modules:
  0.0 226.9 jit_solution(17805520162609653825)
XLA Ops:
  7.9 2.8 %stack.2 = bf16[16,128,576]{1,2,0:T(8,128)(2,1)} broadcast(bf16[128,576]{0,1:T(8,128)(2,1)} %param.5), dimensions={1,2} | broadcast | bytes 2506752 | tf_op jit(solution)/shard_map/stack | solution.py:48
  10.7 6.5 %all-to-all-start = ((bf16[16,128,576]{1,2,0:T(8,128)(2,1)}), bf16[16,128,576]{1,2,0:T(8,128)(2,1)S(1)}, u32[]{:S(2)}, u32[]{:S(2)}) async-start(bf16[16,128,576]{1,2,0:T(8,128)(2,1)} %stack.2), calls=%async_computation | async-start | bytes 4718592 | tf_op jit(solution)/shard_map/all_to_all | solution.py:48
  17.3 1.6 copy.49
  18.9 1.3 copy.52
  20.2 2.4 %copy.45 = bf16[128,4608]{0,1:T(8,128)(2,1)} copy(bf16[128,4608]{1,0:T(8,128)(2,1)} %param.4) | data formatting | bytes 2359296 | tf_op args[0]
  23.9 31.6 %all-to-all-done = bf16[16,128,576]{1,2,0:T(8,128)(2,1)S(1)} async-done(((bf16[16,128,576]{1,2,0:T(8,128)(2,1)}), bf16[16,128,576]{1,2,0:T(8,128)(2,1)S(1)}, u32[]{:S(2)}, u32[]{:S(2)}) %all-to-all-start) | async-done | bytes 2359328 | tf_op jit(solution)/shard_map/all_to_all | solution.py:48
  55.5 2.9 %copy.44 = bf16[16,128,576]{1,0,2:T(8,128)(2,1)} copy(bf16[16,128,576]{1,2,0:T(8,128)(2,1)S(1)} %all-to-all-done) | data formatting | bytes 4718592 | tf_op jit(solution)/shard_map/all_to_all | solution.py:48
  58.5 5.0 %reshape.128 = bf16[2048,576,1]{0,1,2:T(8,128)(2,1)} reshape(bf16[16,128,576]{1,0,2:T(8,128)(2,1)} %copy.44) | data formatting | bytes 4718592 | tf_op jit(solution)/shard_map/reshape | solution.py:47
  63.4 1.8 copy_bitcast_fusion
  65.2 1.9 all-gather.2.cloned.1.call-done
  67.1 6.1 %fusion.7 = (f32[8,128]{1,0:T(8,128)S(1)}, f32[2048,128,8]{1,0,2:T(8,128)S(1)}) fusion(pred[128,2048]{0,1:T(8,128)(4,1)} %broadcast_compare_fusion, bf16[128,8,576]{0,2,1:T(8,128)(2,1)} %bitcast.92, bf16[2048,576]{0,1:T(8,128)(2,1)} %all-gather.2.cloned.1.call-done), kind=kOutput, calls=%fused_computation.12 | convolution fusion | flops 2422209536 | bytes 12193792 | tf_op jit(solution)/shard_map/thd,pd->htp/dot_general | solution.py:32
  73.2 2.2 select_reduce_fusion
  75.5 1.1 copy-done
  76.5 4.7 %fusion.22 = f32[2048,512]{0,1:T(8,128)} fusion(bf16[128,8,512]{0,2,1:T(8,128)(2,1)S(1)} %bitcast.89, f32[2048,128,8]{1,0,2:T(8,128)S(1)} %get-tuple-element.16, f32[8,128]{1,0:T(8,128)S(1)} %log_add_fusion, pred[128,2048]{0,1:T(8,128)(4,1)S(1)} %copy-done.3), kind=kOutput, calls=%fused_computation.27 | convolution fusion | flops 2157969408 | bytes 13897728 | tf_op jit(solution)/shard_map/htp,the->pe/dot_general | solution.py:67
  81.2 9.9 %multiply_reduce_fusion = (f32[128,8]{0,1:T(8,128)S(1)}, bf16[128,8,512]{2,0,1:T(8,128)(2,1)}) fusion(bf16[128,8,512]{2,0,1:T(8,128)(2,1)} %copy.52, bf16[2048,576]{0,1:T(8,128)(2,1)} %copy_bitcast_fusion, bf16[2048,576,1]{0,1,2:T(8,128)(2,1)S(1)} %copy-done.1, bf16[128,8,576]{0,2,1:T(8,128)(2,1)} %bitcast.93, f32[8,128]{1,0:T(8,128)S(1)} %log_add_fusion, ...), kind=kOutput, calls=%fused_computation.36 | convolution fusion | flops 4576508928 | bytes 8003584 | tf_op jit(solution)/shard_map/htp,pe->the/dot_general | solution.py:52
  91.1 7.2 %fusion.1 = bf16[8,128,2048]{1,2,0:T(8,128)(2,1)S(1)} fusion(f32[2048,128,8]{1,0,2:T(8,128)} %copy-done, bf16[128,8,512]{0,2,1:T(8,128)(2,1)S(1)} %bitcast.90, f32[8,128]{1,0:T(8,128)S(1)} %bitcast.96, f32[8,128]{1,0:T(8,128)S(1)} %log_add_fusion, pred[128,2048]{0,1:T(8,128)(4,1)} %broadcast_compare_fusion, bf16[2048,576]{0,1:T(8,128)(2,1)} %all-gather.2.cloned.1.call-done), kind=kOutput, calls=%fused_computation.2 | convolution fusion | flops 2162163712 | bytes 15998976 | tf_op jit(solution)/shard_map/the,pe->htp/dot_general | solution.py:59
  98.4 2.1 copy-done.6
  100.5 4.3 %fusion.8 = f32[2048,576]{0,1:T(8,128)} fusion(f32[2048,512]{0,1:T(8,128)S(1)} %copy-done.7, bf16[8,128,2048]{1,2,0:T(8,128)(2,1)S(1)} %fusion.1, bf16[128,8,576]{0,2,1:T(8,128)(2,1)S(1)} %bitcast.94), kind=kOutput, calls=%fused_computation.14 | convolution fusion | flops 2418278400 | bytes 14286848 | tf_op jit(solution)/shard_map/htp,thd->pd/dot_general | solution.py:64
  104.7 1.2 copy-done.4
  106.6 1.3 copy.56
  107.9 5.5 %multiply_convert_fusion = bf16[8,128,576]{1,2,0:T(8,128)(2,1)S(1)} fusion(bf16[8,128,2048]{1,2,0:T(8,128)(2,1)} %copy-done.6, bf16[2048,576]{0,1:T(8,128)(2,1)} %all-gather.2.cloned.1.call-done), kind=kOutput, calls=%fused_computation.33 | convolution fusion | flops 2417098752 | bytes 7733248 | tf_op jit(solution)/shard_map/htp,pd->thd/dot_general | solution.py:63
  113.4 1.4 copy.57
  114.8 59.4 %reduce-scatter.2.cloned.1.call-done = f32[128,576]{0,1:T(8,128)} async-done(((f32[2048,576]{0,1:T(8,128)}), f32[128,576]{0,1:T(8,128)}) %reduce-scatter.2.cloned.1.call-update) | async-done | bytes 294928 | tf_op jit(solution)/shard_map/reduce_scatter | solution.py:74
  174.2 45.8 %all-reduce.2 = bf16[128,576]{0,1:T(8,128)(2,1)} all-reduce(f32[128,576]{0,1:T(8,128)} %reduce-scatter.2.cloned.1.call-done), channel_id=1, replica_groups=mesh['ctx'=16,'head'=8] {'head'}, use_global_device_ids=true, to_apply=%region_6.7 | all-reduce | flops 73728 | bytes 442368 | tf_op jit(solution)/shard_map/psum | solution.py:75
  (27 shorter events, 2.7 us)
Async XLA Ops:
  7.2 60.0 %all-gather.2.cloned.1.call-start = ((), (), s32[]{:S(2)}) async-start(), calls=%async_computation.2 | async-start | bytes 2506752 | tf_op jit(solution)/shard_map/all_gather | solution.py:41
  10.7 44.8 %all-to-all-start = ((bf16[16,128,576]{1,2,0:T(8,128)(2,1)}), bf16[16,128,576]{1,2,0:T(8,128)(2,1)S(1)}, u32[]{:S(2)}, u32[]{:S(2)}) async-start(bf16[16,128,576]{1,2,0:T(8,128)(2,1)} %stack.2), calls=%async_computation | async-start | bytes 4718592 | tf_op jit(solution)/shard_map/all_to_all | solution.py:48
  17.2 5.4 %copy-start.5 = (s32[16]{0:T(128)S(1)}, s32[16]{0:T(128)}, u32[]{:S(2)}) copy-start(s32[16]{0:T(128)} %param.6) | copy-start | bytes 196
  17.2 157.0 %reduce-scatter.2.cloned.1.call-start = ((), (), s32[]{:S(2)}) async-start(), calls=%async_computation.3 | async-start | bytes 5013504 | tf_op jit(solution)/shard_map/reduce_scatter | solution.py:74
  67.1 6.1 %copy-start.3 = (pred[128,2048]{0,1:T(8,128)(4,1)S(1)}, pred[128,2048]{0,1:T(8,128)(4,1)}, u32[]{:S(2)}) copy-start(pred[128,2048]{0,1:T(8,128)(4,1)} %broadcast_compare_fusion) | copy-start | bytes 786436
  73.2 3.3 %copy-start = (f32[2048,128,8]{1,0,2:T(8,128)}, f32[2048,128,8]{1,0,2:T(8,128)S(1)}, u32[]{:S(2)}) copy-start(f32[2048,128,8]{1,0,2:T(8,128)S(1)} %get-tuple-element.16) | copy-start | bytes 25165828
  76.5 4.7 %copy-start.1 = (bf16[2048,576,1]{0,1,2:T(8,128)(2,1)S(1)}, bf16[2048,576,1]{0,1,2:T(8,128)(2,1)}, u32[]{:S(2)}) copy-start(bf16[2048,576,1]{0,1,2:T(8,128)(2,1)} %reshape.128) | copy-start | bytes 7077892
  91.1 9.3 %copy-start.2 = (bf16[128,4608]{0,1:T(8,128)(2,1)S(1)}, bf16[128,4608]{0,1:T(8,128)(2,1)}, u32[]{:S(2)}) copy-start(bf16[128,4608]{0,1:T(8,128)(2,1)} %copy.45) | copy-start | bytes 3538948
  91.1 9.3 %copy-start.7 = (f32[2048,512]{0,1:T(8,128)S(1)}, f32[2048,512]{0,1:T(8,128)}, u32[]{:S(2)}) copy-start(f32[2048,512]{0,1:T(8,128)} %fusion.22) | copy-start | bytes 12582916
  98.4 2.1 copy-start.6
  104.7 1.2 copy-start.4
Sparse Core Ops, SparseCore 0:
  9.6 57.4 all-gather.1
  104.9 69.2 reduce-scatter.1
